TPU v7x, 512 devices: a whole 4x8x8 slice. The times are simulated.
512 devices in a mesh: seq: 64 (over y, x, core), head: 8 (over z).
Axes of the slice: x: 4, y: 8, z: 8, core: 2. Of those that a mesh axis runs over, the one named last changes fastest.
Arguments:
- query_act: bfloat16 [32768, 4096], P('seq', 'head'), may hold values from -6 to 6
- key_act: bfloat16 [32768, 4096], P('seq', 'head'), may hold values from -6 to 6
- value_act: bfloat16 [32768, 4096], P('seq', 'head'), may hold values from -16 to 16
- upstream: bfloat16 [32768, 4096], P('seq', 'head'), may hold values from -6 to 6
- norm_gain: float32 [4096], P('head'), may hold values from 0.1 to 1.9
Outputs:
- grad_query: bfloat16 [32768, 4096], P('seq', 'head')
- grad_key: bfloat16 [32768, 4096], P('seq', 'head')
- grad_value: bfloat16 [32768, 4096], P('seq', 'head')
All inputs are finite; a program needn't handle non-finite values.
Results may differ from a plain program's by a relative error of at most 0.0058.
Values sent between devices are 32-bit elements; how exact they have to be, the bound alone decides.
A program may use at most 64 MiB of HBM per device.

v0:
```python
import jax
import jax.numpy as jnp
from jax import lax
from jax.sharding import PartitionSpec as P

HEADS = 32
HD = 128
CH = 128


def prefix(array, axis, combine, identity, reverse):
    peers, position = (lax.axis_size(axis), lax.axis_index(axis))
    everything = lax.all_gather(array, axis)
    start = jnp.broadcast_to(jnp.asarray(identity, array.dtype), array.shape)

    def turn(k, before):
        at = peers - 1 - k if reverse else k
        reached = at > position if reverse else at < position
        new = combine(before, everything[at])
        return jnp.where(reached, new, before)

    return lax.fori_loop(0, peers, turn, start)


def add_states(earlier, later):
    return earlier + later


def causal_mask():
    rows = lax.broadcasted_iota(jnp.int32, (CH, CH), 0)
    columns = lax.broadcasted_iota(jnp.int32, (CH, CH), 1)
    return (columns <= rows).astype(jnp.float32)


def block_table(count, before):
    rows = lax.broadcasted_iota(jnp.int32, (count, count), 0)
    columns = lax.broadcasted_iota(jnp.int32, (count, count), 1)
    if before:
        return (columns < rows).astype(jnp.float32)
    return (columns > rows).astype(jnp.float32)


def local_prefix(states):
    table = block_table(states.shape[0], True)
    return jnp.einsum(
        "dc,chij->dhij",
        table,
        states,
        precision=lax.Precision.HIGHEST,
        preferred_element_type=jnp.float32,
    )


def local_suffix(states):
    table = block_table(states.shape[0], False)
    return jnp.einsum(
        "dc,chij->dhij",
        table,
        states,
        precision=lax.Precision.HIGHEST,
        preferred_element_type=jnp.float32,
    )


def on_device(query_act, key_act, value_act, upstream, norm_gain):
    rows_dev = query_act.shape[0]
    heads_dev = query_act.shape[1] // HD
    groups = rows_dev // CH
    block_shape = (groups, CH, heads_dev, HD)
    query_blk = query_act.reshape(block_shape)
    key_blk = key_act.reshape(block_shape)
    value_blk = value_act.reshape(block_shape)
    causal = causal_mask()[None, None]
    kv_group = jnp.einsum("cthi,cthj->chij", key_blk, value_blk, preferred_element_type=jnp.float32)
    kv_total = jnp.sum(kv_group, 0)
    kv_before = prefix(kv_total, "seq", add_states, jnp.zeros_like(kv_total), False)
    kv_state = (kv_before[None] + local_prefix(kv_group)).astype(jnp.bfloat16)
    fwd_scores = (
        jnp.einsum("cthi,cshi->chts", query_blk, key_blk, preferred_element_type=jnp.float32)
        * causal
    ).astype(jnp.bfloat16)
    attention = jnp.einsum(
        "chts,cshj->cthj", fwd_scores, value_blk, preferred_element_type=jnp.float32
    )
    attention = attention + jnp.einsum(
        "cthi,chij->cthj", query_blk, kv_state, preferred_element_type=jnp.float32
    )
    guided = norm_gain.reshape(heads_dev, HD) * upstream.reshape(block_shape).astype(jnp.float32)
    squares, crossed = lax.psum(
        (jnp.sum(attention * attention, (2, 3)), jnp.sum(guided * attention, (2, 3))), "head"
    )
    total_width = HEADS * HD
    inverse = lax.rsqrt(squares / total_width + 1e-06)[:, :, None, None]
    cross_mean = (crossed / total_width)[:, :, None, None]
    grad_attn = (inverse * guided - inverse**3 * cross_mean * attention).astype(jnp.bfloat16)
    back_scores = (
        jnp.einsum("cthj,cshj->chts", grad_attn, value_blk, preferred_element_type=jnp.float32)
        * causal
    ).astype(jnp.bfloat16)
    qd_group = jnp.einsum(
        "cthi,cthj->chij", query_blk, grad_attn, preferred_element_type=jnp.float32
    )
    qd_own = jnp.sum(qd_group, 0)
    qd_after = prefix(qd_own, "seq", add_states, jnp.zeros_like(qd_own), True)
    qd_state = (qd_after[None] + local_suffix(qd_group)).astype(jnp.bfloat16)
    grad_q = jnp.einsum("chts,cshi->cthi", back_scores, key_blk, preferred_element_type=jnp.float32)
    grad_q = grad_q + jnp.einsum(
        "cthj,chij->cthi", grad_attn, kv_state, preferred_element_type=jnp.float32
    )
    grad_k = jnp.einsum(
        "chts,cthi->cshi", back_scores, query_blk, preferred_element_type=jnp.float32
    )
    grad_k = grad_k + jnp.einsum(
        "cshj,chij->cshi", value_blk, qd_state, preferred_element_type=jnp.float32
    )
    grad_v = jnp.einsum(
        "chts,cthj->cshj", fwd_scores, grad_attn, preferred_element_type=jnp.float32
    )
    grad_v = grad_v + jnp.einsum(
        "cshi,chij->cshj", key_blk, qd_state, preferred_element_type=jnp.float32
    )
    out_shape = (rows_dev, heads_dev * HD)
    return (
        grad_q.astype(jnp.bfloat16).reshape(out_shape),
        grad_k.astype(jnp.bfloat16).reshape(out_shape),
        grad_v.astype(jnp.bfloat16).reshape(out_shape),
    )


def solution(mesh):
    in_specs = (P("seq", "head"), P("seq", "head"), P("seq", "head"), P("seq", "head"), P("head"))
    out_specs = (P("seq", "head"), P("seq", "head"), P("seq", "head"))
    return jax.shard_map(
        on_device, mesh=mesh, in_specs=in_specs, out_specs=out_specs, check_vma=False
    )
```

profile of v0, /device:TPU:1, one launch (start us, length us, event | category | flops | bytes accessed | tf_op | source)
XLA Modules:
  0.0 401.7 jit_solution(11878464255792815414)
XLA Ops:
  7.2 1.2 reshape.44
  8.4 1.2 reshape.45
  9.6 2.0 fusion.33
  11.7 1.2 reshape.43
  12.9 2.4 reshape.49
  15.3 1.5 copy.66
  18.1 1.5 convolution_bitcast_fusion.6
  19.7 103.0 %all-gather.5.cloned.1.call-done = f32[256,128,128]{2,1,0:T(8,128)} async-done(((f32[4,128,128]{2,1,0:T(8,128)}), f32[256,128,128]{2,1,0:T(8,128)}) %all-gather.5.cloned.1.call-update) | async-done | bytes 16777232 | tf_op jit(solution)/shard_map/all_gather | solution.py:13
  122.7 68.1 %while.30 = (s32[]{:T(128)}, f32[4,128,128]{2,1,0:T(8,128)S(1)}, s32[]{:T(128)}, f32[64,4,128,128]{3,2,1,0:T(8,128)}, s32[]{:T(128)}, /*index=5*/s32[]{:T(128)}) while((s32[]{:T(128)}, f32[4,128,128]{2,1,0:T(8,128)S(1)}, s32[]{:T(128)}, f32[64,4,128,128]{3,2,1,0:T(8,128)}, s32[]{:T(128)}, /*index=5*/s32[]{:T(128)}) %tuple.88), condition=%wide.region_2.3_spmd.clone, body=%wide.region_1.2_spmd.clone.sunk | while | flops 196612 | bytes 786525 | solution.py:22
  125.9 1.0 add_select_fusion.4
  128.0 1.0 add_select_fusion.4
  130.1 1.0 add_select_fusion.4
  132.3 1.0 add_select_fusion.4
  134.4 1.0 add_select_fusion.4
  136.5 1.0 add_select_fusion.4
  146.1 1.0 add_select_fusion.4
  148.2 1.0 add_select_fusion.4
  150.4 1.0 add_select_fusion.4
  152.5 1.0 add_select_fusion.4
  154.6 1.0 add_select_fusion.4
  156.8 1.0 add_select_fusion.4
  166.3 1.0 add_select_fusion.4
  168.5 1.0 add_select_fusion.4
  170.6 1.0 add_select_fusion.4
  172.7 1.0 add_select_fusion.4
  174.8 1.0 add_select_fusion.4
  177.0 1.0 add_select_fusion.4
  186.5 1.0 add_select_fusion.4
  188.7 1.0 add_select_fusion.4
  190.8 3.0 fusion.3
  194.6 2.8 multiply_reduce_fusion.1
  197.4 14.4 %all-reduce = (f32[4,128]{1,0:T(4,128)S(1)}, f32[4,128]{1,0:T(4,128)S(1)}) all-reduce(f32[4,128]{1,0:T(4,128)S(1)} %get-tuple-element.225, f32[4,128]{1,0:T(4,128)S(1)} %get-tuple-element.224), channel_id=1, replica_groups=mesh['seq'=64,'head'=8] {'head'}, use_global_device_ids=true, to_apply=%region_6.7 | all-reduce | flops 1024 | bytes 8192 | tf_op jit(solution)/shard_map/psum | solution.py:89
  211.8 1.5 subtract_convert_fusion
  213.3 1.3 fusion.34
  215.5 2.5 copy.78
  218.8 1.6 fusion.7
  221.7 1.4 convolution_bitcast_fusion.2
  223.0 2.4 fusion.35
  225.4 93.0 %all-gather.7.cloned.1.call-done = f32[256,128,128]{2,1,0:T(8,128)} async-done(((f32[4,128,128]{2,1,0:T(8,128)}), f32[256,128,128]{2,1,0:T(8,128)}) %all-gather.7.cloned.1.call-update) | async-done | bytes 16777232 | tf_op jit(solution)/shard_map/all_gather | solution.py:13
  318.4 68.5 %while.31 = (s32[]{:T(128)}, f32[4,128,128]{2,1,0:T(8,128)S(1)}, s32[]{:T(128)}, f32[64,4,128,128]{3,2,1,0:T(8,128)}, s32[]{:T(128)}, /*index=5*/s32[]{:T(128)}, s32[]{:T(128)}, s32[]{:T(128)}) while((s32[]{:T(128)}, f32[4,128,128]{2,1,0:T(8,128)S(1)}, s32[]{:T(128)}, f32[64,4,128,128]{3,2,1,0:T(8,128)}, s32[]{:T(128)}, ...), condition=%wide.region_9.10_spmd.clone, body=%wide.region_8.9_spmd.clone.sunk | while | flops 196616 | bytes 786587 | solution.py:22
  320.6 1.0 add_select_fusion.5
  323.8 1.0 add_select_fusion.5
  327.0 1.0 add_select_fusion.5
  331.3 1.0 add_select_fusion.5
  334.5 1.0 add_select_fusion.5
  337.7 1.0 add_select_fusion.5
  340.9 1.0 add_select_fusion.5
  344.1 1.0 add_select_fusion.5
  347.3 1.0 add_select_fusion.5
  351.6 1.0 add_select_fusion.5
  354.8 1.0 add_select_fusion.5
  358.0 1.0 add_select_fusion.5
  361.2 1.0 add_select_fusion.5
  364.5 1.0 add_select_fusion.5
  367.7 1.0 add_select_fusion.5
  371.9 1.0 add_select_fusion.5
  375.2 1.0 add_select_fusion.5
  378.4 1.0 add_select_fusion.5
  381.6 1.0 add_select_fusion.5
  384.8 1.0 add_select_fusion.5
  386.9 2.4 fusion.4
  389.7 1.5 fusion.9
  391.7 1.7 fusion.10
  393.7 1.1 copy_bitcast_fusion
  (111 shorter events, 97.8 us)
Async XLA Ops:
  7.2 187.4 %copy-start.2 = (f32[512]{0:T(512)S(1)}, f32[512]{0:T(512)}, u32[]{:S(2)}) copy-start(f32[512]{0:T(512)} %param.13) | copy-start | bytes 6148
  7.2 115.5 %all-gather.5.cloned.1.call-start = ((), (), s32[]{:S(2)}) async-start(), calls=%async_computation | async-start | bytes 17039360 | tf_op jit(solution)/shard_map/all_gather | solution.py:13
  11.6 306.8 %all-gather.7.cloned.1.call-start = ((), (), s32[]{:S(2)}) async-start(), calls=%async_computation.1 | async-start | bytes 17039360 | tf_op jit(solution)/shard_map/all_gather | solution.py:13
  17.3 0.8 copy-start.1
  193.8 0.8 copy-start
Sparse Core Ops, SparseCore 0:
  11.9 110.7 all-gather.4
  215.6 102.7 all-gather.6
where the time goes:
time: 406 us; the launch traced here: 402 us
  waiting for transfers between devices  196 us (48%)
  other arithmetic  135 us (33%)
  matrix products  22.9 us (6%)
  local copies, waits for them, and re-layouts  15.9 us (4%)
  blocking collectives  14.4 us (4%)
  between operations  14.2 us (3%)
    all_gather x2, waiting for transfers between devices, prefix(): everything = lax.all_gather(array, axis)  196 us
    select_n x128, other arithmetic, turn(): return jnp.where(reached, new, before)  133 us
    psum x1, blocking collectives, on_device(): lax.psum((jnp.sum(attention * attention, (2, 3)), jnp.sum(guided * attent...  14.4 us
  transfers between devices with their start and end apart: 2, of which 2 were waited for; matrix products, arithmetic and copies ran while one was open for 4% of the time, Pallas kernels for 0%

commit v1 on v0

v1 whole, which is shorter than its diff:
```python
import functools

import jax
import jax.numpy as jnp
from jax import lax
from jax.experimental import pallas as pl
from jax.experimental.pallas import tpu as pltpu
from jax.sharding import PartitionSpec as P

HD = 128
CH = 128
NX = 4
MESH = pl.DeviceIdType.MESH
F32 = jnp.float32
BF16 = jnp.bfloat16


def mm(a, b, ca, cb):
    return lax.dot_general(a, b, (((ca,), (cb,)), ((), ())), preferred_element_type=F32)


def kernel(
    ny, nz, width,
    q_ref, k_ref, v_ref, g_ref, gain_ref, dq_ref, dk_ref, dv_ref,
    loc, tot, fs, att, kvs, gvp, ga,
    cbuf, chip, xin, ysrc, ybuf, xret, rbuf, csrc, cret, zsrc, zbuf,
    c_ss, c_rs, x_ss, x_rs, y_ss, y_rs, r_ss, r_rs, e_ss, e_rs, z_ss, z_rs,
):
    groups = q_ref.shape[0] // CH
    heads = q_ref.shape[1] // HD
    half = heads * HD // 2
    part = half // NX
    me = lax.axis_index("seq")
    z = lax.axis_index("head")
    core = lax.rem(me, 2)
    x = lax.rem(me // 2, NX)
    y = me // (2 * NX)
    other = me + 1 - 2 * core

    def at_x(j):
        return {"seq": (y * NX + j) * 2 + core}

    def at_y(j):
        return {"seq": (j * NX + x) * 2 + core}

    barrier = pltpu.get_barrier_semaphore()
    pl.semaphore_signal(barrier, inc=1, device_id={"seq": other}, device_id_type=MESH)
    for d in range(1, NX):
        pl.semaphore_signal(barrier, inc=1, device_id=at_x(lax.rem(x + d, NX)), device_id_type=MESH)
    for d in range(1, ny):
        pl.semaphore_signal(barrier, inc=1, device_id=at_y(lax.rem(y + d, ny)), device_id_type=MESH)
    for d in range(1, nz):
        pl.semaphore_signal(barrier, inc=1, device_id={"head": lax.rem(z + d, nz)}, device_id_type=MESH)

    started = []

    def send(src, dst, ss, rs, to):
        copy = pltpu.make_async_remote_copy(
            src_ref=src, dst_ref=dst, send_sem=ss, recv_sem=rs, device_id=to, device_id_type=MESH
        )
        copy.start()
        started.append(copy)
        return copy

    def blk(ref, c, h):
        return ref[c * CH:(c + 1) * CH, h * HD:(h + 1) * HD]

    row = lax.broadcasted_iota(jnp.int32, (CH, CH), 0)
    col = lax.broadcasted_iota(jnp.int32, (CH, CH), 1)
    causal = col <= row

    def scan(s, reverse, beside):
        mine = pl.ds(pl.multiple_of(core * half, 128), half)
        theirs = pl.ds(pl.multiple_of((1 - core) * half, 128), half)
        c1 = send(tot.at[s, theirs], cbuf.at[s], c_ss.at[s], c_rs.at[s], {"seq": other})
        beside[0]()
        c1.wait_recv()
        chip[s] = tot[s, mine] + cbuf[s]
        xs = []
        for d in range(1, NX):
            j = lax.rem(x + d, NX)
            xs.append(send(
                chip.at[s, pl.ds(pl.multiple_of(j * part, 8), part)], xin.at[s, x],
                x_ss.at[s, d - 1], x_rs.at[s, d - 1], at_x(j),
            ))
        xin[s, x] = chip[s, pl.ds(pl.multiple_of(x * part, 8), part)]
        beside[1]()
        for c in xs:
            c.wait_recv()
        total = xin[s, 0]
        for j in range(1, NX):
            total = total + xin[s, j]
        ysrc[s] = total
        ys = []
        for d in range(1, ny):
            ys.append(send(
                ysrc.at[s], ybuf.at[s, y], y_ss.at[s, d - 1], y_rs.at[s, d - 1],
                at_y(lax.rem(y + d, ny)),
            ))
        ybuf[s, y] = total
        beside[2]()
        for c in ys:
            c.wait_recv()
        run = jnp.zeros((part, HD), F32)
        for j in range(ny):
            reached = j > y if reverse else j < y
            run = run + jnp.where(reached, ybuf[s, j], 0.0)
        order = range(NX - 1, -1, -1) if reverse else range(NX)
        for j in order:
            xret[s, j] = run
            run = run + xin[s, j]
        rs = []
        for d in range(1, NX):
            j = lax.rem(x + d, NX)
            rs.append(send(
                xret.at[s, j], rbuf.at[s, pl.ds(pl.multiple_of(x * part, 8), part)],
                r_ss.at[s, d - 1], r_rs.at[s, d - 1], at_x(j),
            ))
        rbuf[s, pl.ds(pl.multiple_of(x * part, 8), part)] = xret[s, x]
        beside[3]()
        for c in rs:
            c.wait_recv()
        last = core == (0 if reverse else 1)
        csrc[s] = rbuf[s] + jnp.where(last, 0.0, tot[s, mine])
        e = send(csrc.at[s], cret.at[s, mine], e_ss.at[s], e_rs.at[s], {"seq": other})
        cret[s, mine] = rbuf[s] + jnp.where(last, cbuf[s], 0.0)
        e.wait_recv()

    def kv_part(h):
        run = None
        for c in range(groups):
            group = mm(blk(k_ref, c, h), blk(v_ref, c, h), 0, 0)
            if c > 0:
                loc[c, h] = run
            run = group if c == 0 else run + group
        tot[0, h * HD:(h + 1) * HD] = run

    def fwd_part(h):
        for c in range(groups):
            scores = mm(blk(q_ref, c, h), blk(k_ref, c, h), 1, 1)
            scores = jnp.where(causal, scores, 0.0).astype(BF16)
            fs[c, h] = scores
            att[c, h] = mm(scores, blk(v_ref, c, h), 1, 0)

    def guided(c, h):
        return gain_ref[:, h * HD:(h + 1) * HD] * blk(g_ref, c, h).astype(F32)

    for h in range(heads):
        kv_part(h)
    pl.semaphore_wait(barrier, 1 + (NX - 1) + (ny - 1) + (nz - 1))

    def nothing():
        pass

    def fwd_some(lo, hi):
        def go():
            for h in range(lo, hi):
                fwd_part(h)
        return go

    scan(0, False, [nothing, fwd_some(0, heads // 2), fwd_some(heads // 2, heads), nothing])

    for c in range(groups):
        squares = jnp.zeros((CH, HD), F32)
        crossed = jnp.zeros((CH, HD), F32)
        for h in range(heads):
            state = cret[0, h * HD:(h + 1) * HD]
            if c > 0:
                state = state + loc[c, h]
            state = state.astype(BF16)
            kvs[c, h] = state
            a = att[c, h] + mm(blk(q_ref, c, h), state, 1, 0)
            att[c, h] = a
            squares = squares + a * a
            crossed = crossed + guided(c, h) * a
        zsrc[c:c + 1, :] = jnp.sum(squares.T, 0, keepdims=True)
        zsrc[groups + c:groups + c + 1, :] = jnp.sum(crossed.T, 0, keepdims=True)
    zs = []
    for d in range(1, nz):
        zs.append(send(
            zsrc, zbuf.at[z], z_ss.at[d - 1], z_rs.at[d - 1], {"head": lax.rem(z + d, nz)}
        ))
    zbuf[z] = zsrc[...]
    for c in zs:
        c.wait_recv()
    sums = zbuf[0]
    for j in range(1, nz):
        sums = sums + zbuf[j]
    sums = sums * (1.0 / width)
    inverse = lax.rsqrt(sums[:groups] + 1e-06)
    second = inverse * inverse * inverse * sums[groups:]
    run = [None] * heads
    for c in range(groups - 1, -1, -1):
        inv = jnp.broadcast_to(inverse[c:c + 1], (CH, CH)).T
        sec = jnp.broadcast_to(second[c:c + 1], (CH, CH)).T
        for h in range(heads):
            grad = (inv * guided(c, h) - sec * att[c, h]).astype(BF16)
            ga[c, h] = grad
            group = mm(blk(q_ref, c, h), grad, 0, 0)
            if c < groups - 1:
                loc[c, h] = run[h]
            run[h] = group if c == groups - 1 else run[h] + group
    for h in range(heads):
        tot[1, h * HD:(h + 1) * HD] = run[h]

    def back_part(h):
        for c in range(groups):
            grad = ga[c, h]
            back = mm(grad, blk(v_ref, c, h), 1, 1)
            back = jnp.where(causal, back, 0.0).astype(BF16)
            gq = mm(back, blk(k_ref, c, h), 1, 0) + mm(grad, kvs[c, h], 1, 1)
            dq_ref[c * CH:(c + 1) * CH, h * HD:(h + 1) * HD] = gq.astype(BF16)
            att[c, h] = mm(back, blk(q_ref, c, h), 0, 0)
            gvp[c, h] = mm(fs[c, h], grad, 0, 0)

    def back_some(lo, hi):
        def go():
            for h in range(lo, hi):
                back_part(h)
        return go

    scan(1, True, [nothing, back_some(0, heads // 2), back_some(heads // 2, heads), nothing])

    for h in range(heads):
        for c in range(groups):
            state = cret[1, h * HD:(h + 1) * HD]
            if c < groups - 1:
                state = state + loc[c, h]
            state = state.astype(BF16)
            gk = att[c, h] + mm(blk(v_ref, c, h), state, 1, 1)
            dk_ref[c * CH:(c + 1) * CH, h * HD:(h + 1) * HD] = gk.astype(BF16)
            gv = gvp[c, h] + mm(blk(k_ref, c, h), state, 1, 0)
            dv_ref[c * CH:(c + 1) * CH, h * HD:(h + 1) * HD] = gv.astype(BF16)
    for copy in started:
        copy.wait_send()


def solution(mesh):
    ny = mesh.shape["seq"] // (2 * NX)
    nz = mesh.shape["head"]

    def on_device(query, key, value, upstream, gain):
        rows, columns = query.shape
        groups, heads = rows // CH, columns // HD
        half = columns // 2
        part = half // NX
        vmem = pl.BlockSpec(memory_space=pltpu.VMEM)
        out = jax.ShapeDtypeStruct((rows, columns), BF16)
        dma = pltpu.SemaphoreType.DMA
        blocks = (groups, heads, CH, HD)
        return pl.pallas_call(
            functools.partial(kernel, ny, nz, columns * nz),
            name="linear_attention_backward",
            out_shape=(out, out, out),
            in_specs=[vmem] * 5,
            out_specs=(vmem, vmem, vmem),
            scratch_shapes=[
                pltpu.VMEM(blocks, F32),
                pltpu.VMEM((2, columns, HD), F32),
                pltpu.VMEM(blocks, BF16),
                pltpu.VMEM(blocks, F32),
                pltpu.VMEM(blocks, BF16),
                pltpu.VMEM(blocks, F32),
                pltpu.VMEM(blocks, BF16),
                pltpu.VMEM((2, half, HD), F32),
                pltpu.VMEM((2, half, HD), F32),
                pltpu.VMEM((2, NX, part, HD), F32),
                pltpu.VMEM((2, part, HD), F32),
                pltpu.VMEM((2, ny, part, HD), F32),
                pltpu.VMEM((2, NX, part, HD), F32),
                pltpu.VMEM((2, half, HD), F32),
                pltpu.VMEM((2, half, HD), F32),
                pltpu.VMEM((2, columns, HD), F32),
                pltpu.VMEM((2 * groups, CH), F32),
                pltpu.VMEM((nz, 2 * groups, CH), F32),
                dma((2,)), dma((2,)),
                dma((2, NX - 1)), dma((2, NX - 1)),
                dma((2, ny - 1)), dma((2, ny - 1)),
                dma((2, NX - 1)), dma((2, NX - 1)),
                dma((2,)), dma((2,)),
                dma((nz - 1,)), dma((nz - 1,)),
            ],
            compiler_params=pltpu.CompilerParams(
                collective_id=0, has_side_effects=True, vmem_limit_bytes=40 * 1024 * 1024
            ),
        )(query, key, value, upstream, gain.reshape(1, columns))

    spec = P("seq", "head")
    return jax.shard_map(
        on_device, mesh=mesh, in_specs=(spec, spec, spec, spec, P("head")),
        out_specs=(spec, spec, spec), check_vma=False,
    )
```

time: 406 us -> 67.9 us (0.17)
  waiting for transfers between devices: 196 us -> 0 us
  other arithmetic: 135 us -> 0 us
  Pallas kernels: 0 us -> 59.7 us
  matrix products: 22.9 us -> 0 us
  blocking collectives: 14.4 us -> 0 us
  between operations: 14.2 us -> 0.65 us
  local copies, waits for them, and re-layouts: 15.9 us -> 7.22 us
    all_gather x2 -> x0, waiting for transfers between devices: 196 us -> none  [prefix(): everything = lax.all_gather(array, axis)]
    select_n x128 -> x0, other arithmetic: 133 us -> none  [turn(): return jnp.where(reached, new, before)]
    pallas_call x0 -> x1, Pallas kernels: none -> 59.7 us  [on_device(): pl.pallas_call(functools.partial(kernel, ny, nz, columns * nz), name='lin...]
    dot_general x14 -> x0, matrix products: 22.9 us -> none  [the longest x1 3 us: local_prefix(): jnp.einsum('dc,chij->dhij', table, states, precision=lax.Precision.HIGHES...]
    psum x1 -> x0, blocking collectives: 14.4 us -> none  [on_device(): lax.psum((jnp.sum(attention * attention, (2, 3)), jnp.sum(guided * attent...]
    convert_element_type x6 -> x0, local copies, waits for them, and re-layouts: 5.45 us -> none  [the longest x2 3.94 us: on_device(): upstream.reshape(block_shape).astype(jnp.float32)]
    unnamed x7 -> x13, local copies, waits for them, and re-layouts: 2.45 us -> 7.22 us
    reshape x4 -> x0, local copies, waits for them, and re-layouts: 4.61 us -> none  [the longest x1 1.17 us: on_device(): value_blk = value_act.reshape(block_shape)]
  transfers between devices with their start and end apart: 2 -> 0, of which waited for: 2 -> 0; matrix products, arithmetic and copies ran while one was open for 4% -> 0% of each run, Pallas kernels for 0% -> 0%
where the time goes in v1:
time: 67.9 us; the launch traced here: 67.6 us
  Pallas kernels  59.7 us (88%)
  local copies, waits for them, and re-layouts  7.22 us (11%)
    pallas_call x1, Pallas kernels, on_device(): pl.pallas_call(functools.partial(kernel, ny, nz, columns * nz), name='lin...  59.7 us
    unnamed x13, local copies, waits for them, and re-layouts  7.22 us

profile of v1, /device:TPU:1, one launch (start us, length us, event | category | flops | bytes accessed | tf_op | source)
XLA Modules:
  0.0 67.6 jit_solution(7702303208975381968)
XLA Ops:
  0.6 0.0 copy-start
  0.6 1.0 %copy-done = bf16[512,512]{1,0:T(8,128)(2,1)S(1)} copy-done((bf16[512,512]{1,0:T(8,128)(2,1)S(1)}, bf16[512,512]{1,0:T(8,128)(2,1)}, u32[]{:S(2)}) %copy-start) | copy-done | bytes 524312
  1.7 0.0 copy-start.1
  1.7 1.0 %copy-done.1 = bf16[512,512]{1,0:T(8,128)(2,1)S(1)} copy-done((bf16[512,512]{1,0:T(8,128)(2,1)S(1)}, bf16[512,512]{1,0:T(8,128)(2,1)}, u32[]{:S(2)}) %copy-start.1) | copy-done | bytes 524312
  2.7 0.0 copy-start.2
  2.7 1.0 %copy-done.2 = bf16[512,512]{1,0:T(8,128)(2,1)S(1)} copy-done((bf16[512,512]{1,0:T(8,128)(2,1)S(1)}, bf16[512,512]{1,0:T(8,128)(2,1)}, u32[]{:S(2)}) %copy-start.2) | copy-done | bytes 524312
  3.8 0.0 copy-start.3
  3.8 1.0 %copy-done.3 = bf16[512,512]{1,0:T(8,128)(2,1)S(1)} copy-done((bf16[512,512]{1,0:T(8,128)(2,1)S(1)}, bf16[512,512]{1,0:T(8,128)(2,1)}, u32[]{:S(2)}) %copy-start.3) | copy-done | bytes 524312
  4.8 0.0 copy-start.4
  4.8 0.7 %copy-done.4 = f32[512]{0:T(512)S(1)} copy-done((f32[512]{0:T(512)S(1)}, f32[512]{0:T(512)}, u32[]{:S(2)}) %copy-start.4) | copy-done | bytes 2072
  5.5 59.7 %linear_attention_backward.1 = (bf16[512,512]{1,0:T(8,128)(2,1)S(1)}, bf16[512,512]{1,0:T(8,128)(2,1)S(1)}, bf16[512,512]{1,0:T(8,128)(2,1)S(1)}) custom-call(bf16[512,512]{1,0:T(8,128)(2,1)S(1)} %copy-done, bf16[512,512]{1,0:T(8,128)(2,1)S(1)} %copy-done.1, bf16[512,512]{1,0:T(8,128)(2,1)S(1)} %copy-done.2, bf16[512,512]{1,0:T(8,128)(2,1)S(1)} %copy-done.3, ...), custom_call_target="tpu_custom_call" | custom-call | tf_op jit(solution)/shard_map/linear_attention_backward/pallas_call | solution.py:251
  65.2 0.8 %copy.11 = bf16[512,512]{1,0:T(8,128)(2,1)} copy(bf16[512,512]{1,0:T(8,128)(2,1)S(1)} %get-tuple-element.6) | data formatting | bytes 1048576
  66.0 0.8 %copy.12 = bf16[512,512]{1,0:T(8,128)(2,1)} copy(bf16[512,512]{1,0:T(8,128)(2,1)S(1)} %get-tuple-element.7) | data formatting | bytes 1048576
  66.8 0.8 %copy.13 = bf16[512,512]{1,0:T(8,128)(2,1)} copy(bf16[512,512]{1,0:T(8,128)(2,1)S(1)} %get-tuple-element.8) | data formatting | bytes 1048576
Async XLA Ops:
  0.6 1.0 %copy-start = (bf16[512,512]{1,0:T(8,128)(2,1)S(1)}, bf16[512,512]{1,0:T(8,128)(2,1)}, u32[]{:S(2)}) copy-start(bf16[512,512]{1,0:T(8,128)(2,1)} %q_ref.1) | copy-start | bytes 1572868
  1.7 1.0 %copy-start.1 = (bf16[512,512]{1,0:T(8,128)(2,1)S(1)}, bf16[512,512]{1,0:T(8,128)(2,1)}, u32[]{:S(2)}) copy-start(bf16[512,512]{1,0:T(8,128)(2,1)} %k_ref.1) | copy-start | bytes 1572868
  2.7 1.0 %copy-start.2 = (bf16[512,512]{1,0:T(8,128)(2,1)S(1)}, bf16[512,512]{1,0:T(8,128)(2,1)}, u32[]{:S(2)}) copy-start(bf16[512,512]{1,0:T(8,128)(2,1)} %v_ref.1) | copy-start | bytes 1572868
  3.8 1.0 %copy-start.3 = (bf16[512,512]{1,0:T(8,128)(2,1)S(1)}, bf16[512,512]{1,0:T(8,128)(2,1)}, u32[]{:S(2)}) copy-start(bf16[512,512]{1,0:T(8,128)(2,1)} %g_ref.1) | copy-start | bytes 1572868
  4.8 0.7 %copy-start.4 = (f32[512]{0:T(512)S(1)}, f32[512]{0:T(512)}, u32[]{:S(2)}) copy-start(f32[512]{0:T(512)} %param.9) | copy-start | bytes 6148

commit v2 on v1

v2 whole, which is shorter than its diff:
```python
import functools

import jax
import jax.numpy as jnp
from jax import lax
from jax.experimental import pallas as pl
from jax.experimental.pallas import tpu as pltpu
from jax.sharding import PartitionSpec as P

HD = 128
CH = 128
NX = 4
TOGETHER = 1
MESH = pl.DeviceIdType.MESH
F32 = jnp.float32
BF16 = jnp.bfloat16


def mm(a, b, ca, cb):
    return lax.dot_general(a, b, (((ca,), (cb,)), ((), ())), preferred_element_type=F32)


def far_first(n):
    return sorted(range(1, n), key=lambda d: -min(d, n - d))


def kernel(
    ny, nz, width,
    q_hbm, k_hbm, v_hbm, g_hbm, gain_hbm, dq_hbm, dk_hbm, dv_hbm,
    dq_ref, dk_ref, dv_ref, q_ref, k_ref, v_ref, g_ref, gain_ref,
    loc, tot, fs, att, kvs, gvp, ga,
    cbuf, chip, xin, ysrc, ybuf, xret, rbuf, csrc, cret, zsrc, zbuf,
    out_s, in_s, gain_s, c_ss, c_rs, x_ss, x_rs, y_ss, y_rs, r_ss, r_rs, e_ss, e_rs, z_ss, z_rs,
):
    groups = q_ref.shape[0] // CH
    heads = q_ref.shape[1] // HD
    chunks = heads // TOGETHER
    half = TOGETHER * HD // 2
    part = half // NX
    me = lax.axis_index("seq")
    z = lax.axis_index("head")
    core = lax.rem(me, 2)
    x = lax.rem(me // 2, NX)
    y = me // (2 * NX)
    other = me + 1 - 2 * core

    def load(n, src, dst, h):
        cols = slice(h * HD, (h + 1) * HD)
        copy = pltpu.make_async_copy(src.at[:, cols], dst.at[:, cols], in_s.at[n, h])
        copy.start()
        return copy

    loads = {}
    for h in range(heads):
        loads[1, h] = load(1, k_hbm, k_ref, h)
        loads[2, h] = load(2, v_hbm, v_ref, h)
    for h in range(heads):
        loads[0, h] = load(0, q_hbm, q_ref, h)
    for h in range(heads):
        loads[3, h] = load(3, g_hbm, g_ref, h)
    gain_copy = pltpu.make_async_copy(gain_hbm, gain_ref, gain_s)
    gain_copy.start()

    stored = []

    def store(n, src, dst, h):
        cols = slice(h * HD, (h + 1) * HD)
        copy = pltpu.make_async_copy(src.at[:, cols], dst.at[:, cols], out_s.at[n, h])
        copy.start()
        stored.append(copy)

    def at_x(j):
        return {"seq": (y * NX + j) * 2 + core}

    def at_y(j):
        return {"seq": (j * NX + x) * 2 + core}

    barrier = pltpu.get_barrier_semaphore()
    for d in range(1, ny):
        pl.semaphore_signal(barrier, inc=1, device_id=at_y(lax.rem(y + d, ny)), device_id_type=MESH)
    for d in range(1, nz):
        pl.semaphore_signal(barrier, inc=1, device_id={"head": lax.rem(z + d, nz)}, device_id_type=MESH)
    for d in range(1, NX):
        pl.semaphore_signal(barrier, inc=1, device_id=at_x(lax.rem(x + d, NX)), device_id_type=MESH)
    pl.semaphore_signal(barrier, inc=1, device_id={"seq": other}, device_id_type=MESH)

    def send(src, dst, ss, rs, to):
        copy = pltpu.make_async_remote_copy(
            src_ref=src, dst_ref=dst, send_sem=ss, recv_sem=rs, device_id=to, device_id_type=MESH
        )
        copy.start()

    def blk(ref, c, h):
        return ref[c * CH:(c + 1) * CH, h * HD:(h + 1) * HD]

    row = lax.broadcasted_iota(jnp.int32, (CH, CH), 0)
    col = lax.broadcasted_iota(jnp.int32, (CH, CH), 1)
    causal = col <= row
    mine = pl.ds(pl.multiple_of(core * half, half), half)
    theirs = pl.ds(pl.multiple_of((1 - core) * half, half), half)

    def xpart(j):
        return pl.ds(pl.multiple_of(j * part, part), part)

    def arrived(like, sem):
        pltpu.make_async_copy(like, like, sem).wait()

    def spot(h):
        return h // TOGETHER, slice(h % TOGETHER * HD, (h % TOGETHER + 1) * HD)

    def sent(s):
        arrived(cbuf.at[s], c_ss.at[s])
        arrived(xin.at[s, :, pl.ds(0, NX - 1)], x_ss.at[s])
        arrived(ybuf.at[s, :, pl.ds(0, ny - 1)], y_ss.at[s])
        arrived(xret.at[s, :, pl.ds(0, NX - 1)], r_ss.at[s])
        arrived(cbuf.at[s], e_ss.at[s])

    def scan(s, reverse, produce, beside_x, beside_y, consume):
        last = core == (0 if reverse else 1)
        for k in range(chunks):
            produce(k)
            if s == 0 and k == 0:
                pl.semaphore_wait(barrier, 1 + (NX - 1) + (ny - 1) + (nz - 1))
            send(
                tot.at[s, k, theirs], cbuf.at[s, k], c_ss.at[s], c_rs.at[s, k], {"seq": other}
            )
        for k in range(chunks):
            arrived(cbuf.at[s, k], c_rs.at[s, k])
            chip[s, k] = tot[s, k, mine] + cbuf[s, k]
            for d in far_first(NX):
                j = lax.rem(x + d, NX)
                send(
                    chip.at[s, k, xpart(j)], xin.at[s, k, x],
                    x_ss.at[s], x_rs.at[s, k], at_x(j),
                )
            xin[s, k, x] = chip[s, k, xpart(x)]
        beside_x()
        for k in range(chunks):
            arrived(xin.at[s, k, pl.ds(0, NX - 1)], x_rs.at[s, k])
            total = xin[s, k, 0]
            for j in range(1, NX):
                total = total + xin[s, k, j]
            ysrc[s, k] = total
            for d in far_first(ny):
                send(
                    ysrc.at[s, k], ybuf.at[s, k, y], y_ss.at[s], y_rs.at[s, k],
                    at_y(lax.rem(y + d, ny)),
                )
            ybuf[s, k, y] = total
        beside_y()
        for k in range(chunks):
            arrived(ybuf.at[s, k, pl.ds(0, ny - 1)], y_rs.at[s, k])
            run = jnp.zeros((part, HD), F32)
            for j in range(ny):
                reached = j > y if reverse else j < y
                run = run + jnp.where(reached, ybuf[s, k, j], 0.0)
            order = range(NX - 1, -1, -1) if reverse else range(NX)
            for j in order:
                xret[s, k, j] = run
                run = run + xin[s, k, j]
            for d in far_first(NX):
                send(
                    xret.at[s, k, lax.rem(x + d, NX)], rbuf.at[s, k, xpart(x)],
                    r_ss.at[s], r_rs.at[s, k], at_x(lax.rem(x + d, NX)),
                )
            rbuf[s, k, xpart(x)] = xret[s, k, x]
        for k in range(chunks + 1):
            if k < chunks:
                arrived(rbuf.at[s, k, pl.ds(0, (NX - 1) * part)], r_rs.at[s, k])
                csrc[s, k] = rbuf[s, k] + jnp.where(last, 0.0, tot[s, k, mine])
                send(
                    csrc.at[s, k], cret.at[s, k, mine], e_ss.at[s], e_rs.at[s, k], {"seq": other}
                )
                cret[s, k, mine] = rbuf[s, k] + jnp.where(last, cbuf[s, k], 0.0)
            if k > 0:
                arrived(cret.at[s, k - 1, pl.ds(0, half)], e_rs.at[s, k - 1])
                consume(k - 1)

    def kv_part(h):
        loads[1, h].wait()
        loads[2, h].wait()
        run = None
        for c in range(groups):
            group = mm(blk(k_ref, c, h), blk(v_ref, c, h), 0, 0)
            if c > 0:
                loc[c, h] = run
            run = group if c == 0 else run + group
        k, at = spot(h)
        tot[0, k, at] = run

    def fwd_part(h):
        loads[0, h].wait()
        for c in range(groups):
            scores = mm(blk(q_ref, c, h), blk(k_ref, c, h), 1, 1)
            scores = jnp.where(causal, scores, 0.0).astype(BF16)
            fs[c, h] = scores
            att[c, h] = mm(scores, blk(v_ref, c, h), 1, 0)

    def guided(c, h):
        return gain_ref[:, h * HD:(h + 1) * HD] * blk(g_ref, c, h).astype(F32)

    def some(part_of, lo, hi):
        def go():
            for h in range(lo, hi):
                part_of(h)
        return go

    def each(part_of):
        def go(k):
            for h in range(k * TOGETHER, (k + 1) * TOGETHER):
                part_of(h)
        return go

    squares = [jnp.zeros((CH, HD), F32)] * groups
    crossed = [jnp.zeros((CH, HD), F32)] * groups

    def attend(h):
        if h == 0:
            gain_copy.wait()
        loads[3, h].wait()
        for c in range(groups):
            k, at = spot(h)
            state = cret[0, k, at]
            if c > 0:
                state = state + loc[c, h]
            state = state.astype(BF16)
            kvs[c, h] = state
            a = att[c, h] + mm(blk(q_ref, c, h), state, 1, 0)
            att[c, h] = a
            squares[c] = squares[c] + a * a
            crossed[c] = crossed[c] + guided(c, h) * a

    scan(0, False, each(kv_part), some(fwd_part, 0, heads // 2), some(fwd_part, heads // 2, heads), each(attend))

    for c in range(groups):
        zsrc[c:c + 1, :] = jnp.sum(squares[c].T, 0, keepdims=True)
        zsrc[groups + c:groups + c + 1, :] = jnp.sum(crossed[c].T, 0, keepdims=True)
    for d in far_first(nz):
        send(zsrc, zbuf.at[z], z_ss, z_rs, {"head": lax.rem(z + d, nz)})
    zbuf[z] = zsrc[...]
    arrived(zbuf.at[pl.ds(0, nz - 1)], z_rs)
    sums = zbuf[0]
    for j in range(1, nz):
        sums = sums + zbuf[j]
    sums = sums * (1.0 / width)
    inverse = lax.rsqrt(sums[:groups] + 1e-06)
    second = inverse * inverse * inverse * sums[groups:]
    inv = [jnp.broadcast_to(inverse[c:c + 1], (CH, CH)).T for c in range(groups)]
    sec = [jnp.broadcast_to(second[c:c + 1], (CH, CH)).T for c in range(groups)]

    def qd_part(h):
        run = None
        for c in range(groups - 1, -1, -1):
            grad = (inv[c] * guided(c, h) - sec[c] * att[c, h]).astype(BF16)
            ga[c, h] = grad
            group = mm(blk(q_ref, c, h), grad, 0, 0)
            if c < groups - 1:
                loc[c, h] = run
            run = group if c == groups - 1 else run + group
        k, at = spot(h)
        tot[1, k, at] = run

    def back_part(h):
        for c in range(groups):
            grad = ga[c, h]
            back = mm(grad, blk(v_ref, c, h), 1, 1)
            back = jnp.where(causal, back, 0.0).astype(BF16)
            gq = mm(back, blk(k_ref, c, h), 1, 0) + mm(grad, kvs[c, h], 1, 1)
            dq_ref[c * CH:(c + 1) * CH, h * HD:(h + 1) * HD] = gq.astype(BF16)
            att[c, h] = mm(back, blk(q_ref, c, h), 0, 0)
            gvp[c, h] = mm(fs[c, h], grad, 0, 0)
        store(0, dq_ref, dq_hbm, h)

    def finish(h):
        for c in range(groups):
            k, at = spot(h)
            state = cret[1, k, at]
            if c < groups - 1:
                state = state + loc[c, h]
            state = state.astype(BF16)
            gk = att[c, h] + mm(blk(v_ref, c, h), state, 1, 1)
            dk_ref[c * CH:(c + 1) * CH, h * HD:(h + 1) * HD] = gk.astype(BF16)
            gv = gvp[c, h] + mm(blk(k_ref, c, h), state, 1, 0)
            dv_ref[c * CH:(c + 1) * CH, h * HD:(h + 1) * HD] = gv.astype(BF16)
        store(1, dk_ref, dk_hbm, h)
        store(2, dv_ref, dv_hbm, h)

    scan(1, True, each(qd_part), some(back_part, 0, heads // 2), some(back_part, heads // 2, heads), each(finish))
    sent(0)
    sent(1)
    arrived(zbuf.at[pl.ds(0, nz - 1)], z_ss)
    for copy in stored:
        copy.wait()


def write_out(cuts, *refs):
    arrays = (len(refs) - 3) // 2
    held, in_s, out_s = refs[-3:]
    rows = refs[0].shape[0] // cuts
    pieces = [(n, i) for n in range(arrays) for i in range(cuts)]
    reads, writes = {}, []
    for n, i in pieces:
        at = pl.ds(i * rows, rows)
        reads[n, i] = pltpu.make_async_copy(refs[n].at[at], held.at[n, at], in_s.at[n, i])
        reads[n, i].start()
    for n, i in pieces:
        at = pl.ds(i * rows, rows)
        reads[n, i].wait()
        copy = pltpu.make_async_copy(held.at[n, at], refs[arrays + n].at[at], out_s.at[n, i])
        copy.start()
        writes.append(copy)
    for copy in writes:
        copy.wait()


def solution(mesh):
    ny = mesh.shape["seq"] // (2 * NX)
    nz = mesh.shape["head"]

    def on_device(query, key, value, upstream, gain):
        rows, columns = query.shape
        groups, heads = rows // CH, columns // HD
        half = TOGETHER * HD // 2
        part = half // NX
        chunks = heads // TOGETHER
        hbm = pl.BlockSpec(memory_space=pl.ANY)
        out = jax.ShapeDtypeStruct((rows, columns), BF16)
        dma = pltpu.SemaphoreType.DMA
        blocks = (groups, heads, CH, HD)
        whole = pltpu.VMEM((rows, columns), BF16)
        results = pl.pallas_call(
            functools.partial(kernel, ny, nz, columns * nz),
            name="linear_attention_backward",
            out_shape=(out, out, out),
            in_specs=[hbm] * 5,
            out_specs=(hbm, hbm, hbm),
            scratch_shapes=[
                whole, whole, whole,
                whole, whole, whole, whole, pltpu.VMEM((1, columns), F32),
                pltpu.VMEM(blocks, F32),
                pltpu.VMEM((2, chunks, 2 * half, HD), F32),
                pltpu.VMEM(blocks, BF16),
                pltpu.VMEM(blocks, F32),
                pltpu.VMEM(blocks, BF16),
                pltpu.VMEM(blocks, F32),
                pltpu.VMEM(blocks, BF16),
                pltpu.VMEM((2, chunks, half, HD), F32),
                pltpu.VMEM((2, chunks, half, HD), F32),
                pltpu.VMEM((2, chunks, NX, part, HD), F32),
                pltpu.VMEM((2, chunks, part, HD), F32),
                pltpu.VMEM((2, chunks, ny, part, HD), F32),
                pltpu.VMEM((2, chunks, NX, part, HD), F32),
                pltpu.VMEM((2, chunks, half, HD), F32),
                pltpu.VMEM((2, chunks, half, HD), F32),
                pltpu.VMEM((2, chunks, 2 * half, HD), F32),
                pltpu.VMEM((2 * groups, CH), F32),
                pltpu.VMEM((nz, 2 * groups, CH), F32),
                dma((3, heads)), dma((4, heads)), dma,
                dma((2,)), dma((2, chunks)),
                dma((2,)), dma((2, chunks)),
                dma((2,)), dma((2, chunks)),
                dma((2,)), dma((2, chunks)),
                dma((2,)), dma((2, chunks)),
                dma, dma,
            ],
            compiler_params=pltpu.CompilerParams(
                collective_id=0, has_side_effects=True, vmem_limit_bytes=61 * 1024 * 1024
            ),
        )(query, key, value, upstream, gain.reshape(1, columns))
        cuts = 4
        return pl.pallas_call(
            functools.partial(write_out, cuts),
            name="write_out",
            out_shape=(out, out, out),
            in_specs=[hbm] * 3,
            out_specs=(hbm, hbm, hbm),
            scratch_shapes=[
                pltpu.VMEM((3, rows, columns), BF16), dma((3, cuts)), dma((3, cuts)),
            ],
            compiler_params=pltpu.CompilerParams(vmem_limit_bytes=61 * 1024 * 1024),
        )(*results)

    spec = P("seq", "head")
    return jax.shard_map(
        on_device, mesh=mesh, in_specs=(spec, spec, spec, spec, P("head")),
        out_specs=(spec, spec, spec), check_vma=False,
    )
```

time: 67.9 us -> 59.2 us (0.87)
  local copies, waits for them, and re-layouts: 7.22 us -> 0 us
  Pallas kernels: 59.7 us -> 58.4 us
    unnamed x13 -> x0, local copies, waits for them, and re-layouts: 7.22 us -> none
    pallas_call x1, Pallas kernels: 59.7 us -> 56.1 us  [on_device(): pl.pallas_call(functools.partial(kernel, ny, nz, columns * nz), name='lin...]
    pallas_call x0 -> x1, Pallas kernels: none -> 2.33 us  [on_device(): pl.pallas_call(functools.partial(write_out, cuts), name='write_out', out_...]
where the time goes in v2:
time: 59.2 us; the launch traced here: 59.1 us
  Pallas kernels  58.4 us (99%)
  between operations  0.64 us (1%)
    pallas_call x1, Pallas kernels, on_device(): pl.pallas_call(functools.partial(kernel, ny, nz, columns * nz), name='lin...  56.1 us
    pallas_call x1, Pallas kernels, on_device(): pl.pallas_call(functools.partial(write_out, cuts), name='write_out', out_...  2.33 us

profile of v2, /device:TPU:1, one launch (start us, length us, event | category | flops | bytes accessed | tf_op | source)
XLA Modules:
  0.0 59.1 jit_solution(12143387903422378892)
XLA Ops:
  0.6 56.1 %linear_attention_backward.1 = (bf16[512,512]{1,0:T(8,128)(2,1)}, bf16[512,512]{1,0:T(8,128)(2,1)}, bf16[512,512]{1,0:T(8,128)(2,1)}) custom-call(bf16[512,512]{1,0:T(8,128)(2,1)} %q_hbm.1, bf16[512,512]{1,0:T(8,128)(2,1)} %k_hbm.1, bf16[512,512]{1,0:T(8,128)(2,1)} %v_hbm.1, bf16[512,512]{1,0:T(8,128)(2,1)} %g_hbm.1, f32[1,512]{1,0:T(1,128)} %bitcast.1), custom_call_target="tpu_custom_call" | custom-call | tf_op jit(solution)/shard_map/linear_attention_backward/pallas_call | solution.py:331
  56.7 2.3 %write_out.1 = (bf16[512,512]{1,0:T(8,128)(2,1)}, bf16[512,512]{1,0:T(8,128)(2,1)}, bf16[512,512]{1,0:T(8,128)(2,1)}) custom-call(bf16[512,512]{1,0:T(8,128)(2,1)} %get-tuple-element.6.refs_0_, bf16[512,512]{1,0:T(8,128)(2,1)} %get-tuple-element.7.refs_1_, bf16[512,512]{1,0:T(8,128)(2,1)} %get-tuple-element.8.refs_2_), custom_call_target="tpu_custom_call" | custom-call | tf_op jit(solution)/shard_map/write_out/pallas_call | solution.py:371

commit v3 on v2

v3 whole, which is shorter than its diff:
```python
import functools

import jax
import jax.numpy as jnp
from jax import lax
from jax.experimental import pallas as pl
from jax.experimental.pallas import tpu as pltpu
from jax.sharding import PartitionSpec as P

HD = 128
CH = 128
NX = 4
TOGETHER = 1
MESH = pl.DeviceIdType.MESH
F32 = jnp.float32
BF16 = jnp.bfloat16


def mm(a, b, ca, cb):
    return lax.dot_general(a, b, (((ca,), (cb,)), ((), ())), preferred_element_type=F32)


def far_first(n):
    return sorted(range(1, n), key=lambda d: -min(d, n - d))


def kernel(
    ny, nz, width,
    q_hbm, k_hbm, v_hbm, g_hbm, gain_hbm, dq_ref, dk_ref, dv_ref,
    q_ref, k_ref, v_ref, g_ref, gain_ref,
    loc, tot, fs, att, kvs, gvp, ga,
    xin, ysrc, ybuf, xret, cret, zsrc, zbuf,
    in_s, gain_s, x_ss, x_rs, y_ss, y_rs, r_ss, r_rs, z_ss, z_rs,
):
    groups = q_ref.shape[0] // CH
    heads = q_ref.shape[1] // HD
    chunks = heads // TOGETHER
    row_size = 2 * NX
    part = TOGETHER * HD // row_size
    me = lax.axis_index("seq")
    z = lax.axis_index("head")
    core = lax.rem(me, 2)
    x = lax.rem(me // 2, NX)
    y = me // row_size
    rank = lax.rem(me, row_size)
    hops = [(dx, dc) for dx in far_first(NX) for dc in (0, 1)] + [(0, 1)]
    row_peers = [lax.rem(x + dx, NX) * 2 + lax.rem(core + dc, 2) for dx, dc in hops]

    def load(n, src, dst, h):
        cols = slice(h * HD, (h + 1) * HD)
        copy = pltpu.make_async_copy(src.at[:, cols], dst.at[:, cols], in_s.at[n, h])
        copy.start()
        return copy

    loads = {}
    for h in range(heads):
        loads[1, h] = load(1, k_hbm, k_ref, h)
        loads[2, h] = load(2, v_hbm, v_ref, h)
    for h in range(heads):
        loads[0, h] = load(0, q_hbm, q_ref, h)
    for h in range(heads):
        loads[3, h] = load(3, g_hbm, g_ref, h)
    gain_copy = pltpu.make_async_copy(gain_hbm, gain_ref, gain_s)
    gain_copy.start()

    def in_row(j):
        return {"seq": y * row_size + j}

    def at_y(j):
        return {"seq": j * row_size + rank}

    ybuf[...] = jnp.zeros_like(ybuf)
    barrier = pltpu.get_barrier_semaphore()
    for d in range(1, ny):
        pl.semaphore_signal(barrier, inc=1, device_id=at_y(lax.rem(y + d, ny)), device_id_type=MESH)
    for d in range(1, nz):
        pl.semaphore_signal(barrier, inc=1, device_id={"head": lax.rem(z + d, nz)}, device_id_type=MESH)
    for j in row_peers:
        pl.semaphore_signal(barrier, inc=1, device_id=in_row(j), device_id_type=MESH)

    def send(src, dst, ss, rs, to):
        copy = pltpu.make_async_remote_copy(
            src_ref=src, dst_ref=dst, send_sem=ss, recv_sem=rs, device_id=to, device_id_type=MESH
        )
        copy.start()

    def blk(ref, c, h):
        return ref[c * CH:(c + 1) * CH, h * HD:(h + 1) * HD]

    row = lax.broadcasted_iota(jnp.int32, (CH, CH), 0)
    col = lax.broadcasted_iota(jnp.int32, (CH, CH), 1)
    causal = col <= row

    def share(j):
        return pl.ds(pl.multiple_of(j * part, part), part)

    def arrived(like, sem):
        pltpu.make_async_copy(like, like, sem).wait()

    def spot(h):
        return h // TOGETHER, slice(h % TOGETHER * HD, (h % TOGETHER + 1) * HD)

    def sent(s, reverse):
        arrived(xin.at[s, :, pl.ds(0, row_size - 1)], x_ss.at[s])
        for d in range(1, ny):
            to = y - d if reverse else y + d

            @pl.when(jnp.logical_and(to >= 0, to < ny))
            def _(d=d):
                arrived(ysrc.at[s], y_ss.at[s, d - 1])
        arrived(xret.at[s, :, pl.ds(0, row_size - 1)], r_ss.at[s])

    def scan(s, reverse, produce, beside_x, beside_y, consume):
        for k in range(chunks):
            produce(k)
            if s == 0 and k == 0:
                pl.semaphore_wait(barrier, (row_size - 1) + (ny - 1) + (nz - 1))
            for j in row_peers:
                send(tot.at[s, k, share(j)], xin.at[s, k, rank], x_ss.at[s], x_rs.at[s, k], in_row(j))
            xin[s, k, rank] = tot[s, k, share(rank)]
        beside_x()
        for k in range(chunks):
            arrived(xin.at[s, k, pl.ds(0, row_size - 1)], x_rs.at[s, k])
            total = xin[s, k, 0]
            for j in range(1, row_size):
                total = total + xin[s, k, j]
            ysrc[s, k] = total
            for d in far_first(ny):
                to = y - d if reverse else y + d

                @pl.when(jnp.logical_and(to >= 0, to < ny))
                def _(to=to, k=k, d=d):
                    send(
                        ysrc.at[s, k], ybuf.at[s, k, y],
                        y_ss.at[s, d - 1], y_rs.at[s, k, d - 1], at_y(to),
                    )
        beside_y()
        for k in range(chunks):
            for d in range(1, ny):
                source = y + d if reverse else y - d

                @pl.when(jnp.logical_and(source >= 0, source < ny))
                def _(k=k, d=d):
                    arrived(ysrc.at[s, k], y_rs.at[s, k, d - 1])
            run = ybuf[s, k, 0]
            for j in range(1, ny):
                run = run + ybuf[s, k, j]
            order = range(row_size - 1, -1, -1) if reverse else range(row_size)
            for j in order:
                xret[s, k, j] = run
                run = run + xin[s, k, j]
            for j in row_peers:
                send(xret.at[s, k, j], cret.at[s, k, share(rank)], r_ss.at[s], r_rs.at[s, k], in_row(j))
            cret[s, k, share(rank)] = xret[s, k, rank]
        for k in range(chunks):
            arrived(cret.at[s, k, pl.ds(0, (row_size - 1) * part)], r_rs.at[s, k])
            consume(k)

    def kv_part(h):
        loads[1, h].wait()
        loads[2, h].wait()
        run = None
        for c in range(groups):
            group = mm(blk(k_ref, c, h), blk(v_ref, c, h), 0, 0)
            if c > 0:
                loc[c, h] = run
            run = group if c == 0 else run + group
        k, at = spot(h)
        tot[0, k, at] = run

    def fwd_part(h):
        loads[0, h].wait()
        for c in range(groups):
            scores = mm(blk(q_ref, c, h), blk(k_ref, c, h), 1, 1)
            scores = jnp.where(causal, scores, 0.0).astype(BF16)
            fs[c, h] = scores
            att[c, h] = mm(scores, blk(v_ref, c, h), 1, 0)

    def guided(c, h):
        return gain_ref[:, h * HD:(h + 1) * HD] * blk(g_ref, c, h).astype(F32)

    def some(part_of, lo, hi):
        def go():
            for h in range(lo, hi):
                part_of(h)
        return go

    def each(part_of):
        def go(k):
            for h in range(k * TOGETHER, (k + 1) * TOGETHER):
                part_of(h)
        return go

    squares = [jnp.zeros((CH, HD), F32)] * groups
    crossed = [jnp.zeros((CH, HD), F32)] * groups

    def attend(h):
        if h == 0:
            gain_copy.wait()
        loads[3, h].wait()
        for c in range(groups):
            k, at = spot(h)
            state = cret[0, k, at]
            if c > 0:
                state = state + loc[c, h]
            state = state.astype(BF16)
            kvs[c, h] = state
            a = att[c, h] + mm(blk(q_ref, c, h), state, 1, 0)
            att[c, h] = a
            squares[c] = squares[c] + a * a
            crossed[c] = crossed[c] + guided(c, h) * a

    scan(0, False, each(kv_part), some(fwd_part, 0, heads // 2), some(fwd_part, heads // 2, heads), each(attend))

    for c in range(groups):
        zsrc[c:c + 1, :] = jnp.sum(squares[c].T, 0, keepdims=True)
        zsrc[groups + c:groups + c + 1, :] = jnp.sum(crossed[c].T, 0, keepdims=True)
    for d in far_first(nz):
        send(zsrc, zbuf.at[z], z_ss, z_rs, {"head": lax.rem(z + d, nz)})
    zbuf[z] = zsrc[...]
    arrived(zbuf.at[pl.ds(0, nz - 1)], z_rs)
    sums = zbuf[0]
    for j in range(1, nz):
        sums = sums + zbuf[j]
    sums = sums * (1.0 / width)
    inverse = lax.rsqrt(sums[:groups] + 1e-06)
    second = inverse * inverse * inverse * sums[groups:]
    inv = [jnp.broadcast_to(inverse[c:c + 1], (CH, CH)).T for c in range(groups)]
    sec = [jnp.broadcast_to(second[c:c + 1], (CH, CH)).T for c in range(groups)]

    def qd_part(h):
        run = None
        for c in range(groups - 1, -1, -1):
            grad = (inv[c] * guided(c, h) - sec[c] * att[c, h]).astype(BF16)
            ga[c, h] = grad
            group = mm(blk(q_ref, c, h), grad, 0, 0)
            if c < groups - 1:
                loc[c, h] = run
            run = group if c == groups - 1 else run + group
        k, at = spot(h)
        tot[1, k, at] = run

    def back_part(h):
        for c in range(groups):
            grad = ga[c, h]
            back = mm(grad, blk(v_ref, c, h), 1, 1)
            back = jnp.where(causal, back, 0.0).astype(BF16)
            gq = mm(back, blk(k_ref, c, h), 1, 0) + mm(grad, kvs[c, h], 1, 1)
            dq_ref[c * CH:(c + 1) * CH, h * HD:(h + 1) * HD] = gq.astype(BF16)
            att[c, h] = mm(back, blk(q_ref, c, h), 0, 0)
            gvp[c, h] = mm(fs[c, h], grad, 0, 0)

    def finish(h):
        for c in range(groups):
            k, at = spot(h)
            state = cret[1, k, at]
            if c < groups - 1:
                state = state + loc[c, h]
            state = state.astype(BF16)
            gk = att[c, h] + mm(blk(v_ref, c, h), state, 1, 1)
            dk_ref[c * CH:(c + 1) * CH, h * HD:(h + 1) * HD] = gk.astype(BF16)
            gv = gvp[c, h] + mm(blk(k_ref, c, h), state, 1, 0)
            dv_ref[c * CH:(c + 1) * CH, h * HD:(h + 1) * HD] = gv.astype(BF16)

    scan(1, True, each(qd_part), some(back_part, 0, heads // 2), some(back_part, heads // 2, heads), each(finish))
    sent(0, False)
    sent(1, True)
    arrived(zbuf.at[pl.ds(0, nz - 1)], z_ss)


def write_out(cuts, *refs):
    arrays = (len(refs) - 1) // 2
    sems = refs[-1]
    rows = refs[0].shape[0] // cuts
    writes = []
    for n in range(arrays):
        for i in range(cuts):
            at = pl.ds(i * rows, rows)
            writes.append(pltpu.make_async_copy(
                refs[n].at[at], refs[arrays + n].at[at], sems.at[n, i]
            ))
    for copy in writes:
        copy.start()
    for copy in writes:
        copy.wait()


def solution(mesh):
    ny = mesh.shape["seq"] // (2 * NX)
    nz = mesh.shape["head"]

    def on_device(query, key, value, upstream, gain):
        rows, columns = query.shape
        groups, heads = rows // CH, columns // HD
        row_size = 2 * NX
        part = TOGETHER * HD // row_size
        chunks = heads // TOGETHER
        vmem = pl.BlockSpec(memory_space=pltpu.VMEM)
        hbm = pl.BlockSpec(memory_space=pl.ANY)
        out = jax.ShapeDtypeStruct((rows, columns), BF16)
        dma = pltpu.SemaphoreType.DMA
        blocks = (groups, heads, CH, HD)
        whole = pltpu.VMEM((rows, columns), BF16)
        results = pl.pallas_call(
            functools.partial(kernel, ny, nz, columns * nz),
            name="linear_attention_backward",
            out_shape=(whole, whole, whole),
            in_specs=[hbm] * 5,
            out_specs=(vmem, vmem, vmem),
            scratch_shapes=[
                whole, whole, whole, whole, pltpu.VMEM((1, columns), F32),
                pltpu.VMEM(blocks, F32),
                pltpu.VMEM((2, chunks, TOGETHER * HD, HD), F32),
                pltpu.VMEM(blocks, BF16),
                pltpu.VMEM(blocks, F32),
                pltpu.VMEM(blocks, BF16),
                pltpu.VMEM(blocks, F32),
                pltpu.VMEM(blocks, BF16),
                pltpu.VMEM((2, chunks, row_size, part, HD), F32),
                pltpu.VMEM((2, chunks, part, HD), F32),
                pltpu.VMEM((2, chunks, ny, part, HD), F32),
                pltpu.VMEM((2, chunks, row_size, part, HD), F32),
                pltpu.VMEM((2, chunks, TOGETHER * HD, HD), F32),
                pltpu.VMEM((2 * groups, CH), F32),
                pltpu.VMEM((nz, 2 * groups, CH), F32),
                dma((4, heads)), dma,
                dma((2,)), dma((2, chunks)),
                dma((2, ny - 1)), dma((2, chunks, ny - 1)),
                dma((2,)), dma((2, chunks)),
                dma, dma,
            ],
            compiler_params=pltpu.CompilerParams(
                collective_id=0, has_side_effects=True, vmem_limit_bytes=61 * 1024 * 1024
            ),
        )(query, key, value, upstream, gain.reshape(1, columns))
        cuts = 4
        return pl.pallas_call(
            functools.partial(write_out, cuts),
            name="write_out",
            out_shape=(out, out, out),
            in_specs=[vmem] * 3,
            out_specs=(hbm, hbm, hbm),
            scratch_shapes=[dma((3, cuts))],
            compiler_params=pltpu.CompilerParams(vmem_limit_bytes=1024 * 1024),
        )(*results)

    spec = P("seq", "head")
    return jax.shard_map(
        on_device, mesh=mesh, in_specs=(spec, spec, spec, spec, P("head")),
        out_specs=(spec, spec, spec), check_vma=False,
    )
```

time: 59.2 us -> 54.9 us (0.927)
  Pallas kernels: 58.4 us -> 54.1 us
    pallas_call x1, Pallas kernels: 56.1 us -> 52.9 us  [on_device(): pl.pallas_call(functools.partial(kernel, ny, nz, columns * nz), name='lin...]
    pallas_call x1, Pallas kernels: 2.33 us -> 1.24 us  [on_device(): pl.pallas_call(functools.partial(write_out, cuts), name='write_out', out_...]
where the time goes in v3:
time: 54.9 us; the launch traced here: 54.8 us
  Pallas kernels  54.1 us (99%)
  between operations  0.64 us (1%)
    pallas_call x1, Pallas kernels, on_device(): pl.pallas_call(functools.partial(kernel, ny, nz, columns * nz), name='lin...  52.9 us
    pallas_call x1, Pallas kernels, on_device(): pl.pallas_call(functools.partial(write_out, cuts), name='write_out', out_...  1.24 us

profile of v3, /device:TPU:1, one launch (start us, length us, event | category | flops | bytes accessed | tf_op | source)
XLA Modules:
  0.0 54.8 jit_solution(5979127712436792425)
XLA Ops:
  0.6 52.9 %linear_attention_backward.1 = (bf16[512,512]{1,0:T(8,128)(2,1)S(1)}, bf16[512,512]{1,0:T(8,128)(2,1)S(1)}, bf16[512,512]{1,0:T(8,128)(2,1)S(1)}) custom-call(bf16[512,512]{1,0:T(8,128)(2,1)} %q_hbm.1, bf16[512,512]{1,0:T(8,128)(2,1)} %k_hbm.1, bf16[512,512]{1,0:T(8,128)(2,1)} %v_hbm.1, bf16[512,512]{1,0:T(8,128)(2,1)} %g_hbm.1, f32[1,512]{1,0:T(1,128)} %bitcast.1), custom_call_target="tpu_custom_call" | custom-call | tf_op jit(solution)/shard_map/linear_attention_backward/pallas_call | solution.py:304
  53.5 1.2 %write_out.1 = (bf16[512,512]{1,0:T(8,128)(2,1)}, bf16[512,512]{1,0:T(8,128)(2,1)}, bf16[512,512]{1,0:T(8,128)(2,1)}) custom-call(bf16[512,512]{1,0:T(8,128)(2,1)S(1)} %get-tuple-element.6.refs_0_, bf16[512,512]{1,0:T(8,128)(2,1)S(1)} %get-tuple-element.7.refs_1_, bf16[512,512]{1,0:T(8,128)(2,1)S(1)} %get-tuple-element.8.refs_2_), custom_call_target="tpu_custom_call" | custom-call | tf_op jit(solution)/shard_map/write_out/pallas_call | solution.py:337

commit v4 on v3

--- a/solution.py
+++ b/solution.py
@@ -52,6 +52,27 @@
         copy.start()
         return copy
 
+    def in_row(j):
+        return {"seq": y * row_size + j}
+
+    def at_y(j):
+        return {"seq": j * row_size + rank}
+
+    ybuf[...] = jnp.zeros_like(ybuf)
+    barrier = pltpu.get_barrier_semaphore()
+    for d in range(1, ny):
+        pl.semaphore_signal(barrier, inc=1, device_id=at_y(lax.rem(y + d, ny)), device_id_type=MESH)
+    for d in range(1, nz):
+        pl.semaphore_signal(barrier, inc=1, device_id={"head": lax.rem(z + d, nz)}, device_id_type=MESH)
+    for j in row_peers:
+        pl.semaphore_signal(barrier, inc=1, device_id=in_row(j), device_id_type=MESH)
+
+    def send(src, dst, ss, rs, to):
+        copy = pltpu.make_async_remote_copy(
+            src_ref=src, dst_ref=dst, send_sem=ss, recv_sem=rs, device_id=to, device_id_type=MESH
+        )
+        copy.start()
+
     loads = {}
     for h in range(heads):
         loads[1, h] = load(1, k_hbm, k_ref, h)
@@ -63,27 +84,6 @@
     gain_copy = pltpu.make_async_copy(gain_hbm, gain_ref, gain_s)
     gain_copy.start()
 
-    def in_row(j):
-        return {"seq": y * row_size + j}
-
-    def at_y(j):
-        return {"seq": j * row_size + rank}
-
-    ybuf[...] = jnp.zeros_like(ybuf)
-    barrier = pltpu.get_barrier_semaphore()
-    for d in range(1, ny):
-        pl.semaphore_signal(barrier, inc=1, device_id=at_y(lax.rem(y + d, ny)), device_id_type=MESH)
-    for d in range(1, nz):
-        pl.semaphore_signal(barrier, inc=1, device_id={"head": lax.rem(z + d, nz)}, device_id_type=MESH)
-    for j in row_peers:
-        pl.semaphore_signal(barrier, inc=1, device_id=in_row(j), device_id_type=MESH)
-
-    def send(src, dst, ss, rs, to):
-        copy = pltpu.make_async_remote_copy(
-            src_ref=src, dst_ref=dst, send_sem=ss, recv_sem=rs, device_id=to, device_id_type=MESH
-        )
-        copy.start()
-
     def blk(ref, c, h):
         return ref[c * CH:(c + 1) * CH, h * HD:(h + 1) * HD]
 
@@ -111,10 +111,13 @@
         arrived(xret.at[s, :, pl.ds(0, row_size - 1)], r_ss.at[s])
 
     def scan(s, reverse, produce, beside_x, beside_y, consume):
+        if s == 0:
+            for k in range(chunks):
+                produce(k)
+            pl.semaphore_wait(barrier, (row_size - 1) + (ny - 1) + (nz - 1))
         for k in range(chunks):
-            produce(k)
-            if s == 0 and k == 0:
-                pl.semaphore_wait(barrier, (row_size - 1) + (ny - 1) + (nz - 1))
+            if s > 0:
+                produce(k)
             for j in row_peers:
                 send(tot.at[s, k, share(j)], xin.at[s, k, rank], x_ss.at[s], x_rs.at[s, k], in_row(j))
             xin[s, k, rank] = tot[s, k, share(rank)]
@@ -125,7 +128,7 @@
             for j in range(1, row_size):
                 total = total + xin[s, k, j]
             ysrc[s, k] = total
-            for d in far_first(ny):
+            for d in range(ny - 1, 0, -1):
                 to = y - d if reverse else y + d
 
                 @pl.when(jnp.logical_and(to >= 0, to < ny))
@@ -218,6 +221,9 @@
     for d in far_first(nz):
         send(zsrc, zbuf.at[z], z_ss, z_rs, {"head": lax.rem(z + d, nz)})
     zbuf[z] = zsrc[...]
+    for h in range(heads):
+        for c in range(groups):
+            gvp[c, h] = guided(c, h)
     arrived(zbuf.at[pl.ds(0, nz - 1)], z_rs)
     sums = zbuf[0]
     for j in range(1, nz):
@@ -231,7 +237,7 @@
     def qd_part(h):
         run = None
         for c in range(groups - 1, -1, -1):
-            grad = (inv[c] * guided(c, h) - sec[c] * att[c, h]).astype(BF16)
+            grad = (inv[c] * gvp[c, h] - sec[c] * att[c, h]).astype(BF16)
             ga[c, h] = grad
             group = mm(blk(q_ref, c, h), grad, 0, 0)
             if c < groups - 1:
@@ -333,7 +339,7 @@
                 collective_id=0, has_side_effects=True, vmem_limit_bytes=61 * 1024 * 1024
             ),
         )(query, key, value, upstream, gain.reshape(1, columns))
-        cuts = 4
+        cuts = 1
         return pl.pallas_call(
             functools.partial(write_out, cuts),
             name="write_out",

time: 54.9 us -> 54.7 us (level); the launches traced: 54.8 us -> 54 us
  Pallas kernels: 54.1 us -> 53.3 us
    pallas_call x1, Pallas kernels: 52.9 us -> 52.2 us  [on_device(): pl.pallas_call(functools.partial(kernel, ny, nz, columns * nz), name='lin...]
where the time goes in v4:
time: 54.7 us; the launch traced here: 54 us
  Pallas kernels  53.3 us (97%)
  between operations  0.64 us (1%)
    pallas_call x1, Pallas kernels, on_device(): pl.pallas_call(functools.partial(kernel, ny, nz, columns * nz), name='lin...  52.2 us
    pallas_call x1, Pallas kernels, on_device(): pl.pallas_call(functools.partial(write_out, cuts), name='write_out', out_...  1.17 us

profile of v4, /device:TPU:1, one launch (start us, length us, event | category | flops | bytes accessed | tf_op | source)
XLA Modules:
  0.0 54.0 jit_solution(9092093669547122865)
XLA Ops:
  0.6 52.2 %linear_attention_backward.1 = (bf16[512,512]{1,0:T(8,128)(2,1)S(1)}, bf16[512,512]{1,0:T(8,128)(2,1)S(1)}, bf16[512,512]{1,0:T(8,128)(2,1)S(1)}) custom-call(bf16[512,512]{1,0:T(8,128)(2,1)} %q_hbm.1, bf16[512,512]{1,0:T(8,128)(2,1)} %k_hbm.1, bf16[512,512]{1,0:T(8,128)(2,1)} %v_hbm.1, bf16[512,512]{1,0:T(8,128)(2,1)} %g_hbm.1, f32[1,512]{1,0:T(1,128)} %bitcast.1), custom_call_target="tpu_custom_call" | custom-call | tf_op jit(solution)/shard_map/linear_attention_backward/pallas_call | solution.py:310
  52.8 1.2 %write_out.1 = (bf16[512,512]{1,0:T(8,128)(2,1)}, bf16[512,512]{1,0:T(8,128)(2,1)}, bf16[512,512]{1,0:T(8,128)(2,1)}) custom-call(bf16[512,512]{1,0:T(8,128)(2,1)S(1)} %get-tuple-element.6.refs_0_, bf16[512,512]{1,0:T(8,128)(2,1)S(1)} %get-tuple-element.7.refs_1_, bf16[512,512]{1,0:T(8,128)(2,1)S(1)} %get-tuple-element.8.refs_2_), custom_call_target="tpu_custom_call" | custom-call | tf_op jit(solution)/shard_map/write_out/pallas_call | solution.py:343

commit v5 on v4

--- a/solution.py
+++ b/solution.py
@@ -135,16 +135,15 @@
                 def _(to=to, k=k, d=d):
                     send(
                         ysrc.at[s, k], ybuf.at[s, k, y],
-                        y_ss.at[s, d - 1], y_rs.at[s, k, d - 1], at_y(to),
+                        y_ss.at[s, d - 1], y_rs.at[s, k], at_y(to),
                     )
         beside_y()
         for k in range(chunks):
-            for d in range(1, ny):
-                source = y + d if reverse else y - d
-
-                @pl.when(jnp.logical_and(source >= 0, source < ny))
-                def _(k=k, d=d):
-                    arrived(ysrc.at[s, k], y_rs.at[s, k, d - 1])
+            for n in range(1, ny):
+
+                @pl.when((ny - 1 - y if reverse else y) == n)
+                def _(k=k, n=n):
+                    arrived(ybuf.at[s, k, pl.ds(0, n)], y_rs.at[s, k])
             run = ybuf[s, k, 0]
             for j in range(1, ny):
                 run = run + ybuf[s, k, j]
@@ -331,7 +330,7 @@
                 pltpu.VMEM((nz, 2 * groups, CH), F32),
                 dma((4, heads)), dma,
                 dma((2,)), dma((2, chunks)),
-                dma((2, ny - 1)), dma((2, chunks, ny - 1)),
+                dma((2, ny - 1)), dma((2, chunks)),
                 dma((2,)), dma((2, chunks)),
                 dma, dma,
             ],

time: 54.7 us -> 54.3 us (level)
  no operation moved by 1% of the time
where the time goes in v5:
time: 54.3 us; the launch traced here: 53.6 us
  Pallas kernels  52.9 us (97%)
  between operations  0.64 us (1%)
    pallas_call x1, Pallas kernels, on_device(): pl.pallas_call(functools.partial(kernel, ny, nz, columns * nz), name='lin...  51.8 us
    pallas_call x1, Pallas kernels, on_device(): pl.pallas_call(functools.partial(write_out, cuts), name='write_out', out_...  1.17 us

profile of v5, /device:TPU:1, one launch (start us, length us, event | category | flops | bytes accessed | tf_op | source)
XLA Modules:
  0.0 53.6 jit_solution(4791114759167475703)
XLA Ops:
  0.6 51.8 %linear_attention_backward.1 = (bf16[512,512]{1,0:T(8,128)(2,1)S(1)}, bf16[512,512]{1,0:T(8,128)(2,1)S(1)}, bf16[512,512]{1,0:T(8,128)(2,1)S(1)}) custom-call(bf16[512,512]{1,0:T(8,128)(2,1)} %q_hbm.1, bf16[512,512]{1,0:T(8,128)(2,1)} %k_hbm.1, bf16[512,512]{1,0:T(8,128)(2,1)} %v_hbm.1, bf16[512,512]{1,0:T(8,128)(2,1)} %g_hbm.1, f32[1,512]{1,0:T(1,128)} %bitcast.1), custom_call_target="tpu_custom_call" | custom-call | tf_op jit(solution)/shard_map/linear_attention_backward/pallas_call | solution.py:309
  52.4 1.2 %write_out.1 = (bf16[512,512]{1,0:T(8,128)(2,1)}, bf16[512,512]{1,0:T(8,128)(2,1)}, bf16[512,512]{1,0:T(8,128)(2,1)}) custom-call(bf16[512,512]{1,0:T(8,128)(2,1)S(1)} %get-tuple-element.6.refs_0_, bf16[512,512]{1,0:T(8,128)(2,1)S(1)} %get-tuple-element.7.refs_1_, bf16[512,512]{1,0:T(8,128)(2,1)S(1)} %get-tuple-element.8.refs_2_), custom_call_target="tpu_custom_call" | custom-call | tf_op jit(solution)/shard_map/write_out/pallas_call | solution.py:342
